TPU v7x, 256 devices: a whole 4x4x8 slice. The times are simulated.
256 devices in a mesh: energy: 64 (over y, z, x_hi), slab: 4 (over x_lo, core).
Axes of the slice: x: 4 (x_hi: 2, x_lo: 2; x = x_hi * 2 + x_lo), y: 4, z: 8, core: 2. Of those that a mesh axis runs over, the one named last changes fastest.
Arguments:
- lesser: bfloat16 [64, 4, 2, 1024, 1024], P('energy', 'slab'), may hold values from -6 to 6
- greater_diag: float32 [64, 4, 1024], P('energy', 'slab'), may hold values from -6 to 6
- dipole: bfloat16 [4, 1024, 1024], P('slab'), may hold values from -0.1875 to 0.1875
- photon_weights: float32 [64, 3], P('energy'), may hold values from 0.2 to 1
- sidebands: int32 [64], P('energy'), may hold values from 1 to 2
- phonon_lags: int32 [6], replicated, may hold values from 1 to 31
- phonon_strengths: float32 [2, 6], replicated, may hold values from 0.3 to 1.5
- slab_coupling: float32 [4, 1024], P('slab'), may hold values from 0.3 to 1
Outputs:
- lesser_self: bfloat16 [64, 4, 2, 1024, 1024], P('energy', 'slab')
- greater_phonon: float32 [64, 4, 1024], P('energy', 'slab')
All inputs are finite; a program needn't handle non-finite values.
Results may differ from a plain program's by a relative error of at most 0.0057.
Values may be sent and summed in bfloat16 or wider, within the bound.
A program may use at most 64 MiB of HBM per device.

v0:
```python
import jax
import jax.numpy as jnp
from jax import lax
from jax.sharding import PartitionSpec as P

PHOT_BLOCKS = 3


def extended(block, sides, width):
    for axis, dim in sides:
        count = lax.axis_size(axis)
        forward = [(i, i + 1) for i in range(count - 1)]
        backward = [(target, source) for source, target in forward]
        low = lax.ppermute(
            lax.slice_in_dim(block, block.shape[dim] - width, None, axis=dim), axis, forward
        )
        high = lax.ppermute(lax.slice_in_dim(block, 0, width, axis=dim), axis, backward)
        block = jnp.concatenate([low, block, high], axis=dim)
    return block


def shifted(block, axis, distance):
    devices = range(lax.axis_size(axis))
    route = [(i - distance, i) for i in devices if i - distance in devices]
    return lax.ppermute(block, axis, route)


def kernel(rows, cols, phonon_lags, first, second):
    offset = cols[None, :] - rows[:, None]
    upward = (offset[None, :, :] == phonon_lags[:, None, None]).astype(jnp.float32)
    downward = (offset[None, :, :] == -phonon_lags[:, None, None]).astype(jnp.float32)
    return jnp.sum(first[:, None, None] * upward + second[:, None, None] * downward, axis=0)


def left_of(blocks, dipole):
    return jnp.einsum(
        "escij,skj->escik", blocks, dipole, preferred_element_type=jnp.float32
    ).astype(jnp.bfloat16)


def on_device(
    lesser,
    greater_diag,
    dipole,
    photon_weights,
    sidebands,
    phonon_lags,
    phonon_strengths,
    slab_coupling,
):
    e_count = lesser.shape[0]
    width = lesser.shape[-1]
    total_e = e_count * lax.axis_size("energy")
    own_rows = lax.axis_index("energy") * e_count + jnp.arange(e_count, dtype=jnp.int32)
    diag_less = jnp.diagonal(lesser[:, :, 1], axis1=-2, axis2=-1).astype(jnp.float32)
    stacked_diag = jnp.concatenate([diag_less, greater_diag], axis=-1)
    everyone = lax.all_gather(stacked_diag, "energy", axis=0, tiled=True)
    all_rows = jnp.arange(total_e, dtype=jnp.int32)
    k_less = kernel(own_rows, all_rows, phonon_lags, phonon_strengths[0], phonon_strengths[1])
    k_great = kernel(own_rows, all_rows, phonon_lags, phonon_strengths[1], phonon_strengths[0])
    corr_less = jnp.einsum(
        "ef,fsn->esn", k_less, everyone[..., :width], precision=lax.Precision.HIGHEST
    )
    corr_great = jnp.einsum(
        "ef,fsn->esn", k_great, everyone[..., width:], precision=lax.Precision.HIGHEST
    )
    correlated = jnp.concatenate([corr_less, corr_great], axis=-1)
    coupling = jnp.concatenate([slab_coupling, slab_coupling], axis=-1)
    outgoing = jnp.stack([correlated, coupling * correlated])
    rims = extended(outgoing, (("slab", 2),), 1)
    phonon = correlated + rims[1, :, 0:1] + coupling * rims[0, :, 2:3]
    own_left = left_of(lesser, dipole)
    lower = shifted(own_left, "energy", PHOT_BLOCKS)
    upper = shifted(own_left, "energy", -PHOT_BLOCKS)
    weights = photon_weights[:, :, None, None, None, None]
    flags = sidebands.astype(jnp.float32)[:, None, None, None, None]
    mixed = (
        weights[:, 0] * own_left.astype(jnp.float32)
        + flags
        * (weights[:, 1] * lower.astype(jnp.float32) + weights[:, 2] * upper.astype(jnp.float32))
    ).astype(jnp.bfloat16)
    photon = jnp.einsum("sij,escjk->escik", dipole, mixed, preferred_element_type=jnp.float32)
    eye_mask = (jnp.arange(width)[:, None] == jnp.arange(width)[None, :]).astype(jnp.float32)
    photon = photon.at[:, :, 1].add(eye_mask * phonon[..., :width, None])
    return (photon.astype(jnp.bfloat16), phonon[..., width:])


def solution(mesh):
    return jax.shard_map(
        on_device,
        mesh=mesh,
        in_specs=(
            P("energy", "slab", None, None, None),
            P("energy", "slab", None),
            P("slab", None, None),
            P("energy", None),
            P("energy"),
            P(),
            P(),
            P("slab", None),
        ),
        out_specs=(P("energy", "slab", None, None, None), P("energy", "slab", None)),
        check_vma=False,
    )
```

profile of v0, /device:TPU:1, one launch (start us, length us, event | category | flops | bytes accessed | tf_op | source)
XLA Modules:
  0.0 408.2 jit_solution(17339647209610599391)
XLA Ops:
  0.6 0.0 copy-start
  0.6 0.0 copy-start.5
  0.7 1.6 copy-done
  2.2 8.3 %convert_bitcast_fusion = bf16[1,1,2,1024,1024]{3,4,2,0,1:T(8,128)(2,1)} fusion(bf16[1,1,2,1024,1024]{4,3,2,1,0:T(8,128)(2,1)} %param.10, bf16[1,1024,1024]{2,1,0:T(8,128)(2,1)S(1)} %copy-done), kind=kOutput, calls=%fused_computation.13 | convolution fusion | flops 4297064448 | bytes 10485760 | tf_op jit(solution)/shard_map/escij,skj->escik/dot_general | solution.py:36
  10.5 0.0 copy-start.1
  10.5 0.0 copy-start.4
  10.5 0.0 copy-start.3
  10.5 1.4 collective-permute-start.1
  11.9 9.4 %collective-permute-start = (bf16[1,1,2,1024,1024]{3,4,2,0,1:T(8,128)(2,1)}, bf16[1,1,2,1024,1024]{3,4,2,0,1:T(8,128)(2,1)}, u32[]{:S(2)}, u32[]{:S(2)}) collective-permute-start(bf16[1,1,2,1024,1024]{3,4,2,0,1:T(8,128)(2,1)} %convert_bitcast_fusion), channel_id=1, source_target_pairs={{0,12},{4,16},{8,20},{12,24},{16,28},{20,32},{24,36},{28,40},{32,4... | collective-permute-start | bytes 12582920 | tf_op jit(solution)/shard_map/ppermute | solution.py:25
  21.4 0.0 copy-done.5
  21.4 0.0 copy-start.2
  21.4 3.1 slice_bitcast_fusion.1
  24.5 16.3 %gather_fusion = bf16[1024]{0:T(1024)(128)(2,1)S(1)} fusion(bf16[1024,1024]{1,0:T(8,128)(2,1)} %slice_bitcast_fusion.1, s32[1024]{0:T(1024)S(1)} %bitcast.83), kind=kCustom, calls=%fused_computation | custom fusion | bytes 12288 | tf_op jit(solution)/shard_map/jit(diagonal)/gather | solution.py:55
  40.8 0.0 copy-done.1
  40.9 0.0 copy-done.4
  40.9 0.1 fusion.27
  41.0 0.0 copy-done.3
  41.0 305.5 %all_gather.3 = f32[64,1,2048]{2,1,0:T(1,128)S(1)} all-gather(f32[1,1,2048]{2,1,0:T(1,128)S(1)} %pad_maximum_fusion.1), channel_id=1, replica_groups=mesh['energy'=64,'slab'=4] {'energy'}, dimensions={0}, use_global_device_ids=true | all-gather | bytes 532480 | tf_op jit(solution)/shard_map/all_gather | solution.py:57
  346.6 0.3 fusion.18
  346.8 0.3 fusion.15
  347.2 35.3 %collective-permute-start.3 = (f32[2,1,1,2048]{3,2,1,0:T(1,128)S(1)}, f32[2,1,1,2048]{3,2,1,0:T(1,128)S(1)}, u32[]{:S(2)}, u32[]{:S(2)}) collective-permute-start(f32[2,1,1,2048]{3,2,1,0:T(1,128)S(1)} %pad_maximum_fusion), channel_id=1, source_target_pairs={{1,0},{2,1},{3,2},{5,4},{6,5},{7,6},{9,8},{10,9},{11,10},{13,12},{... | collective-permute-start | bytes 49160 | tf_op jit(solution)/shard_map/ppermute | solution.py:17
  382.5 2.6 collective-permute-start.2
  385.1 0.0 copy-done.2
  385.2 0.6 fusion.33
  386.4 0.0 collective-permute-done.3
  386.5 0.0 collective-permute-done.2
  386.5 0.6 fusion.32
  387.1 0.0 collective-permute-done.1
  387.1 0.0 collective-permute-done
  387.1 10.0 %fusion.1 = f32[2,1024,1024]{2,1,0:T(8,128)S(1)} fusion(bf16[1,1,2,1024,1024]{3,4,2,0,1:T(8,128)(2,1)} %collective-permute-done.1, bf16[1,1,2,1024,1024]{3,4,2,0,1:T(8,128)(2,1)} %collective-permute-done, bf16[1,1,2,1024,1024]{3,4,2,0,1:T(8,128)(2,1)} %convert_bitcast_fusion, f32[]{:T(128)} %bitcast.10, f32[]{:T(128)} %bitcast.8, f32[]{:T(128)} %bitcast.7, ...), kind=kOutput, calls=%fused_computation.3 | convolution fusion | flops 4315938816 | bytes 23068688 | tf_op jit(solution)/shard_map/sij,escjk->escik/dot_general | solution.py:82
  397.1 1.7 copy.25
  398.7 0.7 fusion.4
  399.4 2.6 convert_element_type.53
  402.0 6.2 %copy.13 = bf16[1,1,2,1024,1024]{4,3,2,1,0:T(8,128)(2,1)} copy(bf16[1,1,2,1024,1024]{3,4,2,0,1:T(8,128)(2,1)} %convert_element_type.53) | data formatting | bytes 8388608
  (13 shorter events, 0.2 us)
Async XLA Ops:
  0.6 1.6 copy-start
  0.6 20.7 %copy-start.5 = (s32[6]{0:T(128)S(1)}, s32[6]{0:T(128)}, u32[]{:S(2)}) copy-start(s32[6]{0:T(128)} %param.15) | copy-start | bytes 76
  10.5 30.4 %copy-start.1 = (f32[1,1024]{1,0:T(1,128)S(1)}, f32[1,1024]{1,0:T(1,128)}, u32[]{:S(2)}) copy-start(f32[1,1024]{1,0:T(1,128)} %param.17) | copy-start | bytes 12292
  10.5 30.4 %copy-start.4 = (f32[2,6]{1,0:T(2,128)S(1)}, f32[2,6]{1,0:T(2,128)}, u32[]{:S(2)}) copy-start(f32[2,6]{1,0:T(2,128)} %param.16) | copy-start | bytes 148
  10.5 30.5 %copy-start.3 = (f32[1,1,1024]{2,1,0:T(1,128)S(1)}, f32[1,1,1024]{2,1,0:T(1,128)}, u32[]{:S(2)}) copy-start(f32[1,1,1024]{2,1,0:T(1,128)} %param.11) | copy-start | bytes 12292
  10.5 376.6 %collective-permute-start.1 = (bf16[1,1,2,1024,1024]{3,4,2,0,1:T(8,128)(2,1)}, bf16[1,1,2,1024,1024]{3,4,2,0,1:T(8,128)(2,1)}, u32[]{:S(2)}, u32[]{:S(2)}) collective-permute-start(bf16[1,1,2,1024,1024]{3,4,2,0,1:T(8,128)(2,1)} %convert_bitcast_fusion), channel_id=1, source_target_pairs={{12,0},{16,4},{20,8},{24,12},{28,16},{32,20},{36,24},{40,28},{44,3... | collective-permute-start | bytes 12582920 | tf_op jit(solution)/shard_map/ppermute | solution.py:25
  11.9 375.2 %collective-permute-start = (bf16[1,1,2,1024,1024]{3,4,2,0,1:T(8,128)(2,1)}, bf16[1,1,2,1024,1024]{3,4,2,0,1:T(8,128)(2,1)}, u32[]{:S(2)}, u32[]{:S(2)}) collective-permute-start(bf16[1,1,2,1024,1024]{3,4,2,0,1:T(8,128)(2,1)} %convert_bitcast_fusion), channel_id=1, source_target_pairs={{0,12},{4,16},{8,20},{12,24},{16,28},{20,32},{24,36},{28,40},{32,4... | collective-permute-start | bytes 12582920 | tf_op jit(solution)/shard_map/ppermute | solution.py:25
  21.4 363.8 %copy-start.2 = (f32[1,3]{1,0:T(1,128)S(1)}, f32[1,3]{1,0:T(1,128)}, u32[]{:S(2)}) copy-start(f32[1,3]{1,0:T(1,128)} %param.13) | copy-start | bytes 40
  347.2 39.3 %collective-permute-start.3 = (f32[2,1,1,2048]{3,2,1,0:T(1,128)S(1)}, f32[2,1,1,2048]{3,2,1,0:T(1,128)S(1)}, u32[]{:S(2)}, u32[]{:S(2)}) collective-permute-start(f32[2,1,1,2048]{3,2,1,0:T(1,128)S(1)} %pad_maximum_fusion), channel_id=1, source_target_pairs={{1,0},{2,1},{3,2},{5,4},{6,5},{7,6},{9,8},{10,9},{11,10},{13,12},{... | collective-permute-start | bytes 49160 | tf_op jit(solution)/shard_map/ppermute | solution.py:17
  382.5 4.0 collective-permute-start.2
where the time goes:
time: 409 us; the launch traced here: 408 us
  blocking collectives  306 us (75%)
  starting transfers between devices  48.8 us (12%)
  local copies, waits for them, and re-layouts  30.2 us (7%)
  matrix products  18.8 us (5%)
    all_gather x1, blocking collectives, on_device(): everyone = lax.all_gather(stacked_diag, 'energy', axis=0, tiled=True)  306 us
    ppermute x1, starting transfers between devices, extended(): lax.ppermute(lax.slice_in_dim(block, 0, width, axis=dim), axis, backward)  35.3 us
    gather x1, local copies, waits for them, and re-layouts, on_device(): jnp.diagonal(lesser[:, :, 1], axis1=-2, axis2=-1).astype(jnp.float32)  16.3 us
    ppermute x2, starting transfers between devices, shifted(): return lax.ppermute(block, axis, route)  10.9 us
    dot_general x1, matrix products, on_device(): jnp.einsum('sij,escjk->escik', dipole, mixed, preferred_element_type=jnp....  9.97 us
    unnamed x15, local copies, waits for them, and re-layouts  9.44 us
    dot_general x1, matrix products, left_of(): jnp.einsum('escij,skj->escik', blocks, dipole, preferred_element_type=jnp...  8.26 us
  transfers between devices with their start and end apart: 4, of which 0 were waited for; matrix products, arithmetic and copies ran while one was open for 5% of the time, Pallas kernels for 0%

commit v1 on v0

--- a/solution.py
+++ b/solution.py
@@ -54,7 +54,9 @@
     own_rows = lax.axis_index("energy") * e_count + jnp.arange(e_count, dtype=jnp.int32)
     diag_less = jnp.diagonal(lesser[:, :, 1], axis1=-2, axis2=-1).astype(jnp.float32)
     stacked_diag = jnp.concatenate([diag_less, greater_diag], axis=-1)
-    everyone = lax.all_gather(stacked_diag, "energy", axis=0, tiled=True)
+    everyone = jnp.concatenate(
+        lax.all_to_all(jnp.stack([stacked_diag] * lax.axis_size("energy")), "energy", 0, 0), axis=0
+    )
     all_rows = jnp.arange(total_e, dtype=jnp.int32)
     k_less = kernel(own_rows, all_rows, phonon_lags, phonon_strengths[0], phonon_strengths[1])
     k_great = kernel(own_rows, all_rows, phonon_lags, phonon_strengths[1], phonon_strengths[0])

time: 409 us -> 255 us (0.62)
  blocking collectives: 306 us -> 0 us
  waiting for transfers between devices: 0.01 us -> 170 us
  starting transfers between devices: 48.8 us -> 30.7 us
    all_gather x1 -> x0, blocking collectives: 306 us -> none  [on_device(): everyone = lax.all_gather(stacked_diag, 'energy', axis=0, tiled=True)]
    all_to_all x0 -> x1, waiting for transfers between devices: none -> 170 us  [on_device(): lax.all_to_all(jnp.stack([stacked_diag] * lax.axis_size('energy')), 'ener...]
    ppermute x1, starting transfers between devices: 35.3 us -> 3.42 us  [extended(): lax.ppermute(lax.slice_in_dim(block, 0, width, axis=dim), axis, backward)]
    all_to_all x0 -> x1, starting transfers between devices: none -> 14.3 us  [on_device(): lax.all_to_all(jnp.stack([stacked_diag] * lax.axis_size('energy')), 'ener...]
    unnamed x15 -> x17, local copies, waits for them, and re-layouts: 9.44 us -> 9.45 us
  transfers between devices with their start and end apart: 4 -> 5, of which waited for: 0 -> 1; matrix products, arithmetic and copies ran while one was open for 5% -> 8% of each run, Pallas kernels for 0% -> 0%
where the time goes in v1:
time: 255 us; the launch traced here: 254 us
  waiting for transfers between devices  170 us (67%)
  starting transfers between devices  30.7 us (12%)
  local copies, waits for them, and re-layouts  29.6 us (12%)
  matrix products  19 us (7%)
  other arithmetic  3.5 us (1%)
    all_to_all x1, waiting for transfers between devices, on_device(): lax.all_to_all(jnp.stack([stacked_diag] * lax.axis_size('energy')), 'ener...  170 us
    gather x1, local copies, waits for them, and re-layouts, on_device(): jnp.diagonal(lesser[:, :, 1], axis1=-2, axis2=-1).astype(jnp.float32)  16.2 us
    all_to_all x1, starting transfers between devices, on_device(): lax.all_to_all(jnp.stack([stacked_diag] * lax.axis_size('energy')), 'ener...  14.3 us
    ppermute x2, starting transfers between devices, shifted(): return lax.ppermute(block, axis, route)  10.8 us
    dot_general x1, matrix products, on_device(): jnp.einsum('sij,escjk->escik', dipole, mixed, preferred_element_type=jnp....  9.96 us
    unnamed x17, local copies, waits for them, and re-layouts  9.45 us
    dot_general x1, matrix products, left_of(): jnp.einsum('escij,skj->escik', blocks, dipole, preferred_element_type=jnp...  8.51 us
  transfers between devices with their start and end apart: 5, of which 1 were waited for; matrix products, arithmetic and copies ran while one was open for 8% of the time, Pallas kernels for 0%

profile of v1, /device:TPU:1, one launch (start us, length us, event | category | flops | bytes accessed | tf_op | source)
XLA Modules:
  0.0 254.1 jit_solution(8168668929240933080)
XLA Ops:
  0.6 0.0 copy-start
  0.6 0.0 copy-start.1
  0.7 1.6 copy-done
  2.2 8.5 %convert_bitcast_fusion = bf16[1,1,2,1024,1024]{3,4,2,0,1:T(8,128)(2,1)} fusion(bf16[1,1,2,1024,1024]{4,3,2,1,0:T(8,128)(2,1)} %param.10, bf16[1,1024,1024]{2,1,0:T(8,128)(2,1)S(1)} %copy-done), kind=kOutput, calls=%fused_computation.13 | convolution fusion | flops 4297064448 | bytes 10485760 | tf_op jit(solution)/shard_map/escij,skj->escik/dot_general | solution.py:36
  10.7 0.0 copy-start.4
  10.7 1.4 collective-permute-start.1
  12.2 9.4 %collective-permute-start = (bf16[1,1,2,1024,1024]{3,4,2,0,1:T(8,128)(2,1)}, bf16[1,1,2,1024,1024]{3,4,2,0,1:T(8,128)(2,1)}, u32[]{:S(2)}, u32[]{:S(2)}) collective-permute-start(bf16[1,1,2,1024,1024]{3,4,2,0,1:T(8,128)(2,1)} %convert_bitcast_fusion), channel_id=1, source_target_pairs={{0,12},{4,16},{8,20},{12,24},{16,28},{20,32},{24,36},{28,40},{32,4... | collective-permute-start | bytes 12582920 | tf_op jit(solution)/shard_map/ppermute | solution.py:25
  21.6 0.0 copy-done.1
  21.6 0.0 copy-start.6
  21.6 0.0 copy-start.2
  21.6 0.0 copy-start.5
  21.6 0.0 copy-start.3
  21.6 1.5 slice_bitcast_fusion.1
  23.2 16.2 %gather_fusion = bf16[1024]{0:T(1024)(128)(2,1)S(1)} fusion(bf16[1024,1024]{1,0:T(8,128)(2,1)} %slice_bitcast_fusion.1, s32[1024]{0:T(1024)S(1)} %bitcast.85), kind=kCustom, calls=%fused_computation | custom fusion | bytes 12288 | tf_op jit(solution)/shard_map/jit(diagonal)/gather | solution.py:55
  39.4 0.0 copy-done.4
  39.5 1.1 stack.6
  40.5 14.3 %all-to-all-start = ((f32[64,1,1,2048]{3,2,1,0:T(1,128)}), f32[64,1,1,2048]{3,2,1,0:T(1,128)S(1)}, u32[]{:S(2)}, u32[]{:S(2)}) async-start(f32[64,1,1,2048]{3,2,1,0:T(1,128)} %stack.6), calls=%async_computation | async-start | bytes 1048576 | tf_op jit(solution)/shard_map/all_to_all | solution.py:58
  54.9 0.0 copy-done.6
  54.9 0.0 copy-done.2
  54.9 0.0 copy-done.5
  55.0 0.1 fusion.27
  55.1 169.7 %all-to-all-done = f32[64,1,1,2048]{3,2,1,0:T(1,128)S(1)} async-done(((f32[64,1,1,2048]{3,2,1,0:T(1,128)}), f32[64,1,1,2048]{3,2,1,0:T(1,128)S(1)}, u32[]{:S(2)}, u32[]{:S(2)}) %all-to-all-start) | async-done | bytes 524320 | tf_op jit(solution)/shard_map/all_to_all | solution.py:58
  224.8 0.3 fusion.18
  225.1 0.3 fusion.15
  225.5 3.4 %collective-permute-start.3 = (f32[2,1,1,2048]{3,2,1,0:T(1,128)S(1)}, f32[2,1,1,2048]{3,2,1,0:T(1,128)S(1)}, u32[]{:S(2)}, u32[]{:S(2)}) collective-permute-start(f32[2,1,1,2048]{3,2,1,0:T(1,128)S(1)} %pad_maximum_fusion), channel_id=1, source_target_pairs={{1,0},{2,1},{3,2},{5,4},{6,5},{7,6},{9,8},{10,9},{11,10},{13,12},{... | collective-permute-start | bytes 49160 | tf_op jit(solution)/shard_map/ppermute | solution.py:17
  228.9 2.1 collective-permute-start.2
  231.0 0.0 copy-done.3
  231.0 0.6 fusion.33
  232.3 0.0 collective-permute-done.3
  232.4 0.0 collective-permute-done.2
  232.4 0.6 fusion.32
  233.0 0.0 collective-permute-done.1
  233.0 0.0 collective-permute-done
  233.0 10.0 %fusion.1 = f32[2,1024,1024]{2,1,0:T(8,128)S(1)} fusion(bf16[1,1,2,1024,1024]{3,4,2,0,1:T(8,128)(2,1)} %collective-permute-done.1, bf16[1,1,2,1024,1024]{3,4,2,0,1:T(8,128)(2,1)} %collective-permute-done, bf16[1,1,2,1024,1024]{3,4,2,0,1:T(8,128)(2,1)} %convert_bitcast_fusion, f32[]{:T(128)} %bitcast.10, f32[]{:T(128)} %bitcast.8, f32[]{:T(128)} %bitcast.7, ...), kind=kOutput, calls=%fused_computation.3 | convolution fusion | flops 4315938816 | bytes 23068688 | tf_op jit(solution)/shard_map/sij,escjk->escik/dot_general | solution.py:84
  243.0 1.7 copy.24
  244.6 0.7 fusion.4
  245.3 2.6 %convert_element_type.53 = bf16[1,1,2,1024,1024]{3,4,2,0,1:T(8,128)(2,1)} convert(f32[1,1,2,1024,1024]{3,4,2,0,1:T(8,128)S(1)} %fusion.4) | non-fusion elementwise | flops 2097152 | bytes 12582912 | tf_op jit(solution)/shard_map/convert_element_type | solution.py:87
  247.9 6.2 %copy.12 = bf16[1,1,2,1024,1024]{4,3,2,1,0:T(8,128)(2,1)} copy(bf16[1,1,2,1024,1024]{3,4,2,0,1:T(8,128)(2,1)} %convert_element_type.53) | data formatting | bytes 8388608
  (13 shorter events, 0.2 us)
Async XLA Ops:
  0.6 1.6 copy-start
  0.6 21.0 %copy-start.1 = (bf16[1,1,2,1024,1024]{4,3,2,1,0:T(8,128)(2,1)S(1)}, bf16[1,1,2,1024,1024]{4,3,2,1,0:T(8,128)(2,1)}, u32[]{:S(2)}) copy-start(bf16[1,1,2,1024,1024]{4,3,2,1,0:T(8,128)(2,1)} %param.10) | copy-start | bytes 12582916
  10.7 28.7 %copy-start.4 = (f32[1,1,1024]{2,1,0:T(1,128)S(1)}, f32[1,1,1024]{2,1,0:T(1,128)}, u32[]{:S(2)}) copy-start(f32[1,1,1024]{2,1,0:T(1,128)} %param.11) | copy-start | bytes 12292
  10.7 222.3 %collective-permute-start.1 = (bf16[1,1,2,1024,1024]{3,4,2,0,1:T(8,128)(2,1)}, bf16[1,1,2,1024,1024]{3,4,2,0,1:T(8,128)(2,1)}, u32[]{:S(2)}, u32[]{:S(2)}) collective-permute-start(bf16[1,1,2,1024,1024]{3,4,2,0,1:T(8,128)(2,1)} %convert_bitcast_fusion), channel_id=1, source_target_pairs={{12,0},{16,4},{20,8},{24,12},{28,16},{32,20},{36,24},{40,28},{44,3... | collective-permute-start | bytes 12582920 | tf_op jit(solution)/shard_map/ppermute | solution.py:25
  12.2 220.8 %collective-permute-start = (bf16[1,1,2,1024,1024]{3,4,2,0,1:T(8,128)(2,1)}, bf16[1,1,2,1024,1024]{3,4,2,0,1:T(8,128)(2,1)}, u32[]{:S(2)}, u32[]{:S(2)}) collective-permute-start(bf16[1,1,2,1024,1024]{3,4,2,0,1:T(8,128)(2,1)} %convert_bitcast_fusion), channel_id=1, source_target_pairs={{0,12},{4,16},{8,20},{12,24},{16,28},{20,32},{24,36},{28,40},{32,4... | collective-permute-start | bytes 12582920 | tf_op jit(solution)/shard_map/ppermute | solution.py:25
  21.6 33.3 %copy-start.6 = (s32[6]{0:T(128)S(1)}, s32[6]{0:T(128)}, u32[]{:S(2)}) copy-start(s32[6]{0:T(128)} %param.15) | copy-start | bytes 76
  21.6 33.3 %copy-start.2 = (f32[1,1024]{1,0:T(1,128)S(1)}, f32[1,1024]{1,0:T(1,128)}, u32[]{:S(2)}) copy-start(f32[1,1024]{1,0:T(1,128)} %param.17) | copy-start | bytes 12292
  21.6 33.3 %copy-start.5 = (f32[2,6]{1,0:T(2,128)S(1)}, f32[2,6]{1,0:T(2,128)}, u32[]{:S(2)}) copy-start(f32[2,6]{1,0:T(2,128)} %param.16) | copy-start | bytes 148
  21.6 209.4 %copy-start.3 = (f32[1,3]{1,0:T(1,128)S(1)}, f32[1,3]{1,0:T(1,128)}, u32[]{:S(2)}) copy-start(f32[1,3]{1,0:T(1,128)} %param.13) | copy-start | bytes 40
  40.5 184.3 %all-to-all-start = ((f32[64,1,1,2048]{3,2,1,0:T(1,128)}), f32[64,1,1,2048]{3,2,1,0:T(1,128)S(1)}, u32[]{:S(2)}, u32[]{:S(2)}) async-start(f32[64,1,1,2048]{3,2,1,0:T(1,128)} %stack.6), calls=%async_computation | async-start | bytes 1048576 | tf_op jit(solution)/shard_map/all_to_all | solution.py:58
  225.5 6.9 %collective-permute-start.3 = (f32[2,1,1,2048]{3,2,1,0:T(1,128)S(1)}, f32[2,1,1,2048]{3,2,1,0:T(1,128)S(1)}, u32[]{:S(2)}, u32[]{:S(2)}) collective-permute-start(f32[2,1,1,2048]{3,2,1,0:T(1,128)S(1)} %pad_maximum_fusion), channel_id=1, source_target_pairs={{1,0},{2,1},{3,2},{5,4},{6,5},{7,6},{9,8},{10,9},{11,10},{13,12},{... | collective-permute-start | bytes 49160 | tf_op jit(solution)/shard_map/ppermute | solution.py:17
  228.9 3.5 %collective-permute-start.2 = (f32[2,1,1,2048]{3,2,1,0:T(1,128)S(1)}, f32[2,1,1,2048]{3,2,1,0:T(1,128)S(1)}, u32[]{:S(2)}, u32[]{:S(2)}) collective-permute-start(f32[2,1,1,2048]{3,2,1,0:T(1,128)S(1)} %pad_maximum_fusion), channel_id=1, source_target_pairs={{0,1},{1,2},{2,3},{4,5},{5,6},{6,7},{8,9},{9,10},{10,11},{12,13},{... | collective-permute-start | bytes 49160 | tf_op jit(solution)/shard_map/ppermute | solution.py:14
